TPU v7x, 32 devices: a whole 2x2x4 slice. The times are simulated.
32 devices in a mesh: group: 2 (over x), sector: 16 (over z, y, core).
Axes of the slice: x: 2, y: 2, z: 4, core: 2. Of those that a mesh axis runs over, the one named last changes fastest.
Arguments:
- wave: bfloat16 [32, 16, 256, 256], P(('group', 'sector')), parts along dimension 0, may hold values from -6 to 6
- left_ops: bfloat16 [384, 256, 256], P(('group', 'sector')), parts along dimension 0, may hold values from -0.375 to 0.375
- right_ops: bfloat16 [384, 256, 256], P(('group', 'sector')), parts along dimension 0, may hold values from -0.375 to 0.375
- deltas: int32 [384], P(('group', 'sector')), parts along dimension 0, may hold values from -1 to 1, as said below
- counts: int32 [32], P(('group', 'sector')), parts along dimension 0, may hold values from 2 to 12, as said below
Outputs:
- sigma: bfloat16 [32, 16, 256, 256], P(('group', 'sector')), parts along dimension 0
There are 2 independent parts, one for each index of `group`. A program takes and returns all parts, laid end to end along the dimension named above; each array names one. Nothing has to cross between parts.
Inputs may be any that keep to these rules, and one draw needn't show every extreme that they name: `counts`: some sector has exactly 12 live slots in every draw; slots at or beyond a sector's count are unused. Every sector has 2 or more live slots. In each aligned pair of sectors 2i and 2i + 1 at most one has more than 6 live slots, and every other sector has 2 or 3 live slots. `deltas`: slot 0 of every sector reads the sector below it (offset -1) and slot 1 the sector above it (offset +1).
All inputs are finite; a program needn't handle non-finite values.
Results may differ from a plain program's by a relative error of at most 0.0049.
Values may be sent and summed in bfloat16 or wider, within the bound.
A program may use at most 64 MiB of HBM per device.

v0:
```python
import jax
import jax.numpy as jnp
from jax import lax
from jax.sharding import PartitionSpec as P


def extended(cells, sides, width):
    for axis, dim in sides:
        count = lax.axis_size(axis)
        ends = count - 1
        head = lax.slice_in_dim(cells, 0, width, axis=dim)
        tail = lax.slice_in_dim(cells, cells.shape[dim] - width, cells.shape[dim], axis=dim)
        cells = jnp.concatenate(
            [
                lax.ppermute(tail, axis, [(i, (i + 1) % count) for i in range(ends)]),
                cells,
                lax.ppermute(head, axis, [((i + 1) % count, i) for i in range(ends)]),
            ],
            axis=dim,
        )
    return cells


def apply_pairs(sources, left_ops, right_ops, deltas, offset, last_slot):
    roots_here = sources.shape[1]
    width = sources.shape[2]

    def add_pair(slot_index, running):
        where_from = deltas[slot_index] + offset
        source_block = lax.dynamic_index_in_dim(sources, where_from, 0, keepdims=False)
        left_op = lax.dynamic_index_in_dim(left_ops, slot_index, 0, keepdims=False)
        right_op = lax.dynamic_index_in_dim(right_ops, slot_index, 0, keepdims=False)
        mixed = jnp.einsum(
            "ij,rjk->rik", left_op, source_block, preferred_element_type=jnp.float32
        ).astype(jnp.bfloat16)
        return running + jnp.einsum(
            "rik,lk->ril", mixed, right_op, preferred_element_type=jnp.float32
        )

    empty = jnp.zeros((roots_here, width, width), jnp.float32)
    return lax.fori_loop(jnp.int32(0), last_slot, add_pair, empty)


def on_device(wave, left_ops, right_ops, deltas, counts):
    sources = extended(wave, (("sector", 0),), 1)
    own_count = counts[0]
    running = apply_pairs(sources, left_ops, right_ops, deltas, 1, own_count)
    return running.astype(jnp.bfloat16)[None]


def solution(mesh):
    return jax.shard_map(
        on_device,
        mesh=mesh,
        in_specs=(
            P(("group", "sector"), None, None, None),
            P(("group", "sector"), None, None),
            P(("group", "sector"), None, None),
            P(("group", "sector")),
            P(("group", "sector")),
        ),
        out_specs=P(("group", "sector"), None, None, None),
        check_vma=False,
    )
```

profile of v0, /device:TPU:14, one launch (start us, length us, event | category | flops | bytes accessed | tf_op | source)
XLA Modules:
  0.0 165.3 jit_solution(6876253183321466080)
XLA Ops:
  0.0 1.9 %collective-permute-start = (bf16[1,16,256,256]{3,2,1,0:T(8,128)(2,1)}, bf16[1,16,256,256]{3,2,1,0:T(8,128)(2,1)S(1)}, u32[]{:S(2)}, u32[]{:S(2)}) collective-permute-start(bf16[1,16,256,256]{3,2,1,0:T(8,128)(2,1)} %param.7), channel_id=1, source_target_pairs={{0,1},{1,2},{2,3},{3,4},{4,5},{5,6},{6,7},{7,8},{8,9},{9,10},{10,1... | collective-permute-start | bytes 6291464 | tf_op jit(solution)/shard_map/ppermute | solution.py:15
  1.9 3.6 %collective-permute-start.1 = (bf16[1,16,256,256]{3,2,1,0:T(8,128)(2,1)}, bf16[1,16,256,256]{3,2,1,0:T(8,128)(2,1)}, u32[]{:S(2)}, u32[]{:S(2)}) collective-permute-start(bf16[1,16,256,256]{3,2,1,0:T(8,128)(2,1)} %param.7), channel_id=1, source_target_pairs={{1,0},{2,1},{3,2},{4,3},{5,4},{6,5},{7,6},{8,7},{9,8},{10,9},{11,1... | collective-permute-start | bytes 6291464 | tf_op jit(solution)/shard_map/ppermute | solution.py:17
  5.6 44.5 %collective-permute-done = bf16[1,16,256,256]{3,2,1,0:T(8,128)(2,1)S(1)} collective-permute-done((bf16[1,16,256,256]{3,2,1,0:T(8,128)(2,1)}, bf16[1,16,256,256]{3,2,1,0:T(8,128)(2,1)S(1)}, u32[]{:S(2)}, u32[]{:S(2)}) %collective-permute-start) | collective-permute-done | bytes 2097184 | tf_op jit(solution)/shard_map/ppermute | solution.py:15
  50.0 0.0 collective-permute-done.1
  50.0 5.5 %pad_maximum_fusion = bf16[3,16,256,256]{3,2,1,0:T(8,128)(2,1)} fusion(bf16[1,16,256,256]{3,2,1,0:T(8,128)(2,1)} %collective-permute-done.1, bf16[1,16,256,256]{3,2,1,0:T(8,128)(2,1)} %param.7, bf16[1,16,256,256]{3,2,1,0:T(8,128)(2,1)S(1)} %collective-permute-done), kind=kLoop, calls=%fused_computation.11 | loop fusion | flops 6291456 | bytes 12582912 | tf_op jit(solution)/shard_map/concatenate | solution.py:13
  55.5 0.0 copy-start
  55.5 2.5 %broadcast_in_dim.6 = f32[16,256,256]{2,1,0:T(8,128)} broadcast(f32[]{:T(128)} %constant.37.clone.1), dimensions={} | broadcast | bytes 4194308 | tf_op jit(solution)/shard_map/broadcast_in_dim | solution.py:40
  58.0 0.0 copy-done
  58.0 103.5 %while.12 = (s32[]{:T(128)}, f32[16,256,256]{2,1,0:T(8,128)}, s32[]{:T(128)}, s32[12]{0:T(128)S(1)}, bf16[3,16,256,256]{3,2,1,0:T(8,128)(2,1)}, /*index=5*/bf16[...) while((s32[]{:T(128)}, f32[16,256,256]{2,1,0:T(8,128)}, ...), condition=%wide.region_1.2_spmd, body=%wide.region_0.1_spmd.sunk | while | flops 1075838976 | bytes 10749657 | solution.py:41
  58.7 0.6 dynamic_slice.47
  60.4 6.2 %convolution_add_fusion.2 = f32[16,256,256]{2,1,0:T(8,128)} fusion(f32[16,256,256]{2,1,0:T(8,128)} %get-tuple-element.169, bf16[3,16,256,256]{3,2,1,0:T(8,128)(2,1)} %get-tuple-element.184, s32[]{:T(128)S(6)} %select_n.19, bf16[12,256,256]{2,1,0:T(8,128)(2,1)} %get-tuple-element.186, s32[]{:T(128)S(6)} %select_n.18, ...), kind=kOutput, calls=%fused_computation.clone.1 | convolution fusion | flops 1075838976 | bytes 10749440 | tf_op jit(solution)/shard_map/while/body/rik,lk->ril/dot_general | solution.py:36
  67.2 0.6 dynamic_slice.47
  68.9 6.2 %convolution_add_fusion.2 = f32[16,256,256]{2,1,0:T(8,128)} fusion(f32[16,256,256]{2,1,0:T(8,128)} %get-tuple-element.169, bf16[3,16,256,256]{3,2,1,0:T(8,128)(2,1)} %get-tuple-element.184, s32[]{:T(128)S(6)} %select_n.19, bf16[12,256,256]{2,1,0:T(8,128)(2,1)} %get-tuple-element.186, s32[]{:T(128)S(6)} %select_n.18, ...), kind=kOutput, calls=%fused_computation.clone.1 | convolution fusion | flops 1075838976 | bytes 10749440 | tf_op jit(solution)/shard_map/while/body/rik,lk->ril/dot_general | solution.py:36
  75.8 0.6 dynamic_slice.47
  77.5 6.2 %convolution_add_fusion.2 = f32[16,256,256]{2,1,0:T(8,128)} fusion(f32[16,256,256]{2,1,0:T(8,128)} %get-tuple-element.169, bf16[3,16,256,256]{3,2,1,0:T(8,128)(2,1)} %get-tuple-element.184, s32[]{:T(128)S(6)} %select_n.19, bf16[12,256,256]{2,1,0:T(8,128)(2,1)} %get-tuple-element.186, s32[]{:T(128)S(6)} %select_n.18, ...), kind=kOutput, calls=%fused_computation.clone.1 | convolution fusion | flops 1075838976 | bytes 10749440 | tf_op jit(solution)/shard_map/while/body/rik,lk->ril/dot_general | solution.py:36
  84.4 0.6 dynamic_slice.47
  86.1 6.2 %convolution_add_fusion.2 = f32[16,256,256]{2,1,0:T(8,128)} fusion(f32[16,256,256]{2,1,0:T(8,128)} %get-tuple-element.169, bf16[3,16,256,256]{3,2,1,0:T(8,128)(2,1)} %get-tuple-element.184, s32[]{:T(128)S(6)} %select_n.19, bf16[12,256,256]{2,1,0:T(8,128)(2,1)} %get-tuple-element.186, s32[]{:T(128)S(6)} %select_n.18, ...), kind=kOutput, calls=%fused_computation.clone.1 | convolution fusion | flops 1075838976 | bytes 10749440 | tf_op jit(solution)/shard_map/while/body/rik,lk->ril/dot_general | solution.py:36
  92.9 0.6 dynamic_slice.47
  94.6 6.2 %convolution_add_fusion.2 = f32[16,256,256]{2,1,0:T(8,128)} fusion(f32[16,256,256]{2,1,0:T(8,128)} %get-tuple-element.169, bf16[3,16,256,256]{3,2,1,0:T(8,128)(2,1)} %get-tuple-element.184, s32[]{:T(128)S(6)} %select_n.19, bf16[12,256,256]{2,1,0:T(8,128)(2,1)} %get-tuple-element.186, s32[]{:T(128)S(6)} %select_n.18, ...), kind=kOutput, calls=%fused_computation.clone.1 | convolution fusion | flops 1075838976 | bytes 10749440 | tf_op jit(solution)/shard_map/while/body/rik,lk->ril/dot_general | solution.py:36
  101.5 0.6 dynamic_slice.47
  103.2 6.2 %convolution_add_fusion.2 = f32[16,256,256]{2,1,0:T(8,128)} fusion(f32[16,256,256]{2,1,0:T(8,128)} %get-tuple-element.169, bf16[3,16,256,256]{3,2,1,0:T(8,128)(2,1)} %get-tuple-element.184, s32[]{:T(128)S(6)} %select_n.19, bf16[12,256,256]{2,1,0:T(8,128)(2,1)} %get-tuple-element.186, s32[]{:T(128)S(6)} %select_n.18, ...), kind=kOutput, calls=%fused_computation.clone.1 | convolution fusion | flops 1075838976 | bytes 10749440 | tf_op jit(solution)/shard_map/while/body/rik,lk->ril/dot_general | solution.py:36
  110.1 0.6 dynamic_slice.47
  111.8 6.2 %convolution_add_fusion.2 = f32[16,256,256]{2,1,0:T(8,128)} fusion(f32[16,256,256]{2,1,0:T(8,128)} %get-tuple-element.169, bf16[3,16,256,256]{3,2,1,0:T(8,128)(2,1)} %get-tuple-element.184, s32[]{:T(128)S(6)} %select_n.19, bf16[12,256,256]{2,1,0:T(8,128)(2,1)} %get-tuple-element.186, s32[]{:T(128)S(6)} %select_n.18, ...), kind=kOutput, calls=%fused_computation.clone.1 | convolution fusion | flops 1075838976 | bytes 10749440 | tf_op jit(solution)/shard_map/while/body/rik,lk->ril/dot_general | solution.py:36
  118.6 0.6 dynamic_slice.47
  120.4 6.2 %convolution_add_fusion.2 = f32[16,256,256]{2,1,0:T(8,128)} fusion(f32[16,256,256]{2,1,0:T(8,128)} %get-tuple-element.169, bf16[3,16,256,256]{3,2,1,0:T(8,128)(2,1)} %get-tuple-element.184, s32[]{:T(128)S(6)} %select_n.19, bf16[12,256,256]{2,1,0:T(8,128)(2,1)} %get-tuple-element.186, s32[]{:T(128)S(6)} %select_n.18, ...), kind=kOutput, calls=%fused_computation.clone.1 | convolution fusion | flops 1075838976 | bytes 10749440 | tf_op jit(solution)/shard_map/while/body/rik,lk->ril/dot_general | solution.py:36
  127.2 0.6 dynamic_slice.47
  128.9 6.2 %convolution_add_fusion.2 = f32[16,256,256]{2,1,0:T(8,128)} fusion(f32[16,256,256]{2,1,0:T(8,128)} %get-tuple-element.169, bf16[3,16,256,256]{3,2,1,0:T(8,128)(2,1)} %get-tuple-element.184, s32[]{:T(128)S(6)} %select_n.19, bf16[12,256,256]{2,1,0:T(8,128)(2,1)} %get-tuple-element.186, s32[]{:T(128)S(6)} %select_n.18, ...), kind=kOutput, calls=%fused_computation.clone.1 | convolution fusion | flops 1075838976 | bytes 10749440 | tf_op jit(solution)/shard_map/while/body/rik,lk->ril/dot_general | solution.py:36
  135.8 0.6 dynamic_slice.47
  137.5 6.2 %convolution_add_fusion.2 = f32[16,256,256]{2,1,0:T(8,128)} fusion(f32[16,256,256]{2,1,0:T(8,128)} %get-tuple-element.169, bf16[3,16,256,256]{3,2,1,0:T(8,128)(2,1)} %get-tuple-element.184, s32[]{:T(128)S(6)} %select_n.19, bf16[12,256,256]{2,1,0:T(8,128)(2,1)} %get-tuple-element.186, s32[]{:T(128)S(6)} %select_n.18, ...), kind=kOutput, calls=%fused_computation.clone.1 | convolution fusion | flops 1075838976 | bytes 10749440 | tf_op jit(solution)/shard_map/while/body/rik,lk->ril/dot_general | solution.py:36
  144.4 0.6 dynamic_slice.47
  146.1 6.2 %convolution_add_fusion.2 = f32[16,256,256]{2,1,0:T(8,128)} fusion(f32[16,256,256]{2,1,0:T(8,128)} %get-tuple-element.169, bf16[3,16,256,256]{3,2,1,0:T(8,128)(2,1)} %get-tuple-element.184, s32[]{:T(128)S(6)} %select_n.19, bf16[12,256,256]{2,1,0:T(8,128)(2,1)} %get-tuple-element.186, s32[]{:T(128)S(6)} %select_n.18, ...), kind=kOutput, calls=%fused_computation.clone.1 | convolution fusion | flops 1075838976 | bytes 10749440 | tf_op jit(solution)/shard_map/while/body/rik,lk->ril/dot_general | solution.py:36
  152.9 0.6 dynamic_slice.47
  154.6 6.2 %convolution_add_fusion.2 = f32[16,256,256]{2,1,0:T(8,128)} fusion(f32[16,256,256]{2,1,0:T(8,128)} %get-tuple-element.169, bf16[3,16,256,256]{3,2,1,0:T(8,128)(2,1)} %get-tuple-element.184, s32[]{:T(128)S(6)} %select_n.19, bf16[12,256,256]{2,1,0:T(8,128)(2,1)} %get-tuple-element.186, s32[]{:T(128)S(6)} %select_n.18, ...), kind=kOutput, calls=%fused_computation.clone.1 | convolution fusion | flops 1075838976 | bytes 10749440 | tf_op jit(solution)/shard_map/while/body/rik,lk->ril/dot_general | solution.py:36
  161.5 3.8 %convert_bitcast_fusion = bf16[1,16,256,256]{3,2,1,0:T(8,128)(2,1)} fusion(f32[16,256,256]{2,1,0:T(8,128)} %get-tuple-element.97), kind=kLoop, calls=%fused_computation.12 | loop fusion | flops 1048576 | bytes 6291456 | tf_op jit(solution)/shard_map/broadcast_in_dim | solution.py:48
Async XLA Ops:
  0.0 50.0 %collective-permute-start = (bf16[1,16,256,256]{3,2,1,0:T(8,128)(2,1)}, bf16[1,16,256,256]{3,2,1,0:T(8,128)(2,1)S(1)}, u32[]{:S(2)}, u32[]{:S(2)}) collective-permute-start(bf16[1,16,256,256]{3,2,1,0:T(8,128)(2,1)} %param.7), channel_id=1, source_target_pairs={{0,1},{1,2},{2,3},{3,4},{4,5},{5,6},{6,7},{7,8},{8,9},{9,10},{10,1... | collective-permute-start | bytes 6291464 | tf_op jit(solution)/shard_map/ppermute | solution.py:15
  1.9 48.1 %collective-permute-start.1 = (bf16[1,16,256,256]{3,2,1,0:T(8,128)(2,1)}, bf16[1,16,256,256]{3,2,1,0:T(8,128)(2,1)}, u32[]{:S(2)}, u32[]{:S(2)}) collective-permute-start(bf16[1,16,256,256]{3,2,1,0:T(8,128)(2,1)} %param.7), channel_id=1, source_target_pairs={{1,0},{2,1},{3,2},{4,3},{5,4},{6,5},{7,6},{8,7},{9,8},{10,9},{11,1... | collective-permute-start | bytes 6291464 | tf_op jit(solution)/shard_map/ppermute | solution.py:17
  55.5 2.5 %copy-start = (s32[12]{0:T(128)S(1)}, s32[12]{0:T(128)}, u32[]{:S(2)}) copy-start(s32[12]{0:T(128)} %param.10) | copy-start | bytes 148
where the time goes:
time: 167 us; the launch traced here: 165 us
  matrix products  74.3 us (44%)
  waiting for transfers between devices  44.5 us (27%)
  loops' own time  22.2 us (13%)
  local copies, waits for them, and re-layouts  9.44 us (6%)
  other arithmetic  9.27 us (6%)
  starting transfers between devices  5.55 us (3%)
    dot_general x12, matrix products, add_pair(): jnp.einsum('rik,lk->ril', mixed, right_op, preferred_element_type=jnp.flo...  74.3 us
    ppermute x1, waiting for transfers between devices, extended(): lax.ppermute(tail, axis, [(i, (i + 1) % count) for i in range(ends)])  44.5 us
    another operation x1, loops' own time, apply_pairs(): return lax.fori_loop(jnp.int32(0), last_slot, add_pair, empty)  22.2 us
    dynamic_slice x12, local copies, waits for them, and re-layouts, add_pair(): where_from = deltas[slot_index] + offset  6.99 us
    concatenate x1, other arithmetic, extended(): jnp.concatenate([lax.ppermute(tail, axis, [(i, (i + 1) % count) for i in...  5.5 us
    broadcast_in_dim x1, other arithmetic, on_device(): return running.astype(jnp.bfloat16)[None]  3.77 us
    ppermute x1, starting transfers between devices, extended(): lax.ppermute(head, axis, [((i + 1) % count, i) for i in range(ends)])  3.64 us
  transfers between devices with their start and end apart: 2, of which 1 were waited for; matrix products, arithmetic and copies ran while one was open for 0% of the time, Pallas kernels for 0%

commit v1 on v0

v1 whole, which is shorter than its diff:
```python
import functools

import jax
import jax.numpy as jnp
from jax import lax
from jax.experimental import pallas as pl
from jax.experimental.pallas import tpu as pltpu
from jax.sharding import PartitionSpec as P

MESH = pl.DeviceIdType.MESH


def kernel(
    sectors, counts_ref, deltas_ref, wave_ref, left_ref, right_ref, out_ref,
    own, low, high, left, right, right_t, stage, mixed, result,
    send_sem, low_sem, high_sem, own_sem, op_sem, out_sem,
):
    roots, width = own.shape[0], own.shape[1]
    slots = left.shape[0]
    me = lax.axis_index("sector")
    has_low, has_high = me > 0, me < sectors - 1

    barrier = pltpu.get_barrier_semaphore()

    @pl.when(has_low)
    def _():
        pl.semaphore_signal(barrier, inc=1, device_id={"sector": me - 1}, device_id_type=MESH)

    @pl.when(has_high)
    def _():
        pl.semaphore_signal(barrier, inc=1, device_id={"sector": me + 1}, device_id_type=MESH)

    left_copy = pltpu.make_async_copy(left_ref, left, op_sem.at[0])
    right_copy = pltpu.make_async_copy(right_ref, right, op_sem.at[1])
    own_copy = pltpu.make_async_copy(wave_ref, own, own_sem)
    left_copy.start()
    right_copy.start()
    own_copy.start()

    pl.semaphore_wait(barrier, has_low.astype(jnp.int32) + has_high.astype(jnp.int32))

    def up(root):
        return pltpu.make_async_remote_copy(
            src_ref=wave_ref.at[root], dst_ref=low.at[root],
            send_sem=send_sem.at[0, root], recv_sem=low_sem.at[root],
            device_id={"sector": me + 1}, device_id_type=MESH,
        )

    def down(root):
        return pltpu.make_async_remote_copy(
            src_ref=wave_ref.at[root], dst_ref=high.at[root],
            send_sem=send_sem.at[1, root], recv_sem=high_sem.at[root],
            device_id={"sector": me - 1}, device_id_type=MESH,
        )

    @pl.loop(0, roots)
    def _(root):
        @pl.when(has_high)
        def _():
            up(root).start()

        @pl.when(has_low)
        def _():
            down(root).start()

    @pl.when(jnp.logical_not(has_low))
    def _():
        low[...] = jnp.zeros_like(low)

    @pl.when(jnp.logical_not(has_high))
    def _():
        high[...] = jnp.zeros_like(high)

    left_copy.wait()
    right_copy.wait()
    count = counts_ref[0]

    @pl.loop(0, slots)
    def _(slot):
        live = jnp.where(slot < count, 1.0, 0.0).astype(jnp.float32)
        left[slot] = (left[slot].astype(jnp.float32) * live).astype(left.dtype)
        right_t[pl.ds(pl.multiple_of(slot * width, width), width), :] = right[slot].T

    own_copy.wait()

    def out_copy(root, slot):
        return pltpu.make_async_copy(result.at[slot], out_ref.at[root], out_sem.at[slot])

    @pl.loop(0, roots)
    def _(root):
        @pl.when(has_low)
        def _():
            up(root).wait_recv()

        @pl.when(has_high)
        def _():
            down(root).wait_recv()

        stage[0] = low[root]
        stage[1] = own[root]
        stage[2] = high[root]
        for slot in range(slots):
            source = stage[deltas_ref[slot] + 1]
            mixed[:, slot * width:(slot + 1) * width] = jnp.dot(
                left[slot], source, preferred_element_type=jnp.float32
            ).astype(mixed.dtype)
        total = jnp.dot(mixed[...], right_t[...], preferred_element_type=jnp.float32)
        now = lax.rem(root, 2)

        @pl.when(root >= 2)
        def _():
            out_copy(root - 2, now).wait()

        result[now] = total.astype(result.dtype)
        out_copy(root, now).start()

    for root in (roots - 2, roots - 1):
        out_copy(root, root % 2).wait()

    @pl.loop(0, roots)
    def _(root):
        @pl.when(has_high)
        def _():
            up(root).wait_send()

        @pl.when(has_low)
        def _():
            down(root).wait_send()


def on_device(sectors, wave, left_ops, right_ops, deltas, counts):
    wave = wave[0]
    roots, width = wave.shape[0], wave.shape[1]
    slots = left_ops.shape[0]
    block = (roots, width, width)
    bf16 = wave.dtype
    flops = 4 * roots * slots * width**3
    sigma = pl.pallas_call(
        functools.partial(kernel, sectors),
        out_shape=jax.ShapeDtypeStruct(block, bf16),
        in_specs=[pl.BlockSpec(memory_space=pltpu.SMEM)] * 2 + [pl.BlockSpec(memory_space=pl.ANY)] * 3,
        out_specs=pl.BlockSpec(memory_space=pl.ANY),
        scratch_shapes=[
            pltpu.VMEM(block, bf16),
            pltpu.VMEM(block, bf16),
            pltpu.VMEM(block, bf16),
            pltpu.VMEM((slots, width, width), bf16),
            pltpu.VMEM((slots, width, width), bf16),
            pltpu.VMEM((slots * width, width), bf16),
            pltpu.VMEM((3, width, width), bf16),
            pltpu.VMEM((width, slots * width), bf16),
            pltpu.VMEM((2, width, width), bf16),
            pltpu.SemaphoreType.DMA((2, roots)),
            pltpu.SemaphoreType.DMA((roots,)),
            pltpu.SemaphoreType.DMA((roots,)),
            pltpu.SemaphoreType.DMA,
            pltpu.SemaphoreType.DMA((2,)),
            pltpu.SemaphoreType.DMA((2,)),
        ],
        compiler_params=pltpu.CompilerParams(
            collective_id=0, has_side_effects=True, vmem_limit_bytes=60 * 2**20
        ),
        cost_estimate=pl.CostEstimate(flops=flops, bytes_accessed=7 * 2**20, transcendentals=0),
    )(counts, deltas, wave, left_ops, right_ops)
    return sigma[None]


def solution(mesh):
    return jax.shard_map(
        functools.partial(on_device, mesh.shape["sector"]),
        mesh=mesh,
        in_specs=(
            P(("group", "sector"), None, None, None),
            P(("group", "sector"), None, None),
            P(("group", "sector"), None, None),
            P(("group", "sector")),
            P(("group", "sector")),
        ),
        out_specs=P(("group", "sector"), None, None, None),
        check_vma=False,
    )
```

time: 167 us -> 55.4 us (0.33)
  the two profiles are of different devices: /device:TPU:14 before, /device:TPU:9 now
where the time goes in v1:
time: 55.4 us; the launch traced here: 55.2 us
  Pallas kernels  51.4 us (93%)
  local copies, waits for them, and re-layouts  3.1 us (6%)
  between operations  0.66 us (1%)
    pallas_call x1, Pallas kernels, on_device(): pl.pallas_call(functools.partial(kernel, sectors), out_shape=jax.ShapeDty...  51.4 us
    unnamed x1, local copies, waits for them, and re-layouts  3.1 us

profile of v1, /device:TPU:9, one launch (start us, length us, event | category | flops | bytes accessed | tf_op | source)
XLA Modules:
  0.0 55.2 jit_solution(13627465047044726370)
XLA Ops:
  0.7 51.4 %shard_map.55 = bf16[16,256,256]{2,1,0:T(8,128)(2,1)} custom-call(s32[1]{0:T(128)S(6)} %copy.7.counts_ref, s32[12]{0:T(128)} %deltas_ref.1, bf16[16,256,256]{2,1,0:T(8,128)(2,1)} %bitcast.3, bf16[12,256,256]{2,1,0:T(8,128)(2,1)} %left_ref.1, bf16[12,256,256]{2,1,0:T(8,128)(2,1)} %right_ref.1), custom_call_target="tpu_custom_call" | custom-call | flops 12884901888 | bytes 7340032 | tf_op jit(solution)/shard_map/pallas_call | solution.py:138
  52.1 3.1 %copy.8 = bf16[1,16,256,256]{3,2,1,0:T(8,128)(2,1)} copy(bf16[1,16,256,256]{3,2,1,0:T(8,128)(2,1)} %bitcast.2) | data formatting | bytes 4194304

commit v2 on v1

--- a/solution.py
+++ b/solution.py
@@ -12,23 +12,41 @@
 
 def kernel(
     sectors, counts_ref, deltas_ref, wave_ref, left_ref, right_ref, out_ref,
-    own, low, high, left, right, right_t, stage, mixed, result,
-    send_sem, low_sem, high_sem, own_sem, op_sem, out_sem,
+    own, low, high, passing, left, right, right_t, stage, mixed, result,
+    send_sem, low_sem, high_sem, passing_sem, forward_sem, own_sem, op_sem, out_sem,
 ):
     roots, width = own.shape[0], own.shape[1]
     slots = left.shape[0]
     me = lax.axis_index("sector")
     has_low, has_high = me > 0, me < sectors - 1
 
+    rows = sectors // 4 if sectors == 16 else 0
+    row, place = lax.div(me, 4), lax.rem(me, 4)
+    above, below = row < rows - 1, jnp.logical_and(row > 0, row < rows)
+    up_source = jnp.logical_and(place == 3, above)
+    up_relay = jnp.logical_and(place == 1, above)
+    down_source = jnp.logical_and(place == 0, below)
+    down_relay = jnp.logical_and(place == 2, below)
+    up_share = lax.div(roots * (rows - 1 - row), max(rows, 1))
+    down_share = lax.div(roots * row, max(rows, 1))
+    up_detour = jnp.where(up_source, up_share, 0)
+    down_detour = jnp.where(down_source, down_share, 0)
+    forwards = jnp.where(up_relay, up_share, jnp.where(down_relay, down_share, 0))
+    ahead = jnp.where(up_relay, me + 3, jnp.where(down_relay, me - 3, me))
+
+    partners = [(has_low, me - 1), (has_high, me + 1)]
+    if rows:
+        partners += [
+            (up_source, me - 2), (up_source, me + 3),
+            (down_source, me + 2), (down_source, me - 3),
+            (up_relay, me + 2), (up_relay, me + 3),
+            (down_relay, me - 2), (down_relay, me - 3),
+        ]
     barrier = pltpu.get_barrier_semaphore()
-
-    @pl.when(has_low)
-    def _():
-        pl.semaphore_signal(barrier, inc=1, device_id={"sector": me - 1}, device_id_type=MESH)
-
-    @pl.when(has_high)
-    def _():
-        pl.semaphore_signal(barrier, inc=1, device_id={"sector": me + 1}, device_id_type=MESH)
+    for present, partner in partners:
+        @pl.when(present)
+        def _(partner=partner):
+            pl.semaphore_signal(barrier, inc=1, device_id={"sector": partner}, device_id_type=MESH)
 
     left_copy = pltpu.make_async_copy(left_ref, left, op_sem.at[0])
     right_copy = pltpu.make_async_copy(right_ref, right, op_sem.at[1])
@@ -36,8 +54,7 @@
     left_copy.start()
     right_copy.start()
     own_copy.start()
-
-    pl.semaphore_wait(barrier, has_low.astype(jnp.int32) + has_high.astype(jnp.int32))
+    pl.semaphore_wait(barrier, sum(present.astype(jnp.int32) for present, _ in partners))
 
     def up(root):
         return pltpu.make_async_remote_copy(
@@ -53,15 +70,39 @@
             device_id={"sector": me - 1}, device_id_type=MESH,
         )
 
+    def aside(root, step, way, corner):
+        return pltpu.make_async_remote_copy(
+            src_ref=wave_ref.at[root], dst_ref=passing.at[step],
+            send_sem=send_sem.at[way, root], recv_sem=passing_sem.at[step],
+            device_id={"sector": corner}, device_id_type=MESH,
+        )
+
+    def forward(step, target, target_sem):
+        root = roots - forwards + step
+        return pltpu.make_async_remote_copy(
+            src_ref=passing.at[step], dst_ref=target.at[root],
+            send_sem=forward_sem.at[step], recv_sem=target_sem.at[root],
+            device_id={"sector": ahead}, device_id_type=MESH,
+        )
+
     @pl.loop(0, roots)
-    def _(root):
-        @pl.when(has_high)
-        def _():
-            up(root).start()
-
-        @pl.when(has_low)
-        def _():
-            down(root).start()
+    def _(step):
+        @pl.when(jnp.logical_and(has_high, step < roots - up_detour))
+        def _():
+            up(step).start()
+
+        @pl.when(jnp.logical_and(has_low, step < roots - down_detour))
+        def _():
+            down(step).start()
+
+        if rows:
+            @pl.when(step < up_detour)
+            def _():
+                aside(roots - up_detour + step, step, 0, me - 2).start()
+
+            @pl.when(step < down_detour)
+            def _():
+                aside(roots - down_detour + step, step, 1, me + 2).start()
 
     @pl.when(jnp.logical_not(has_low))
     def _():
@@ -114,6 +155,19 @@
         result[now] = total.astype(result.dtype)
         out_copy(root, now).start()
 
+        if rows:
+            @pl.when(root < forwards)
+            def _():
+                aside(root, root, 0, me).wait_recv()
+
+                @pl.when(up_relay)
+                def _():
+                    forward(root, low, low_sem).start()
+
+                @pl.when(down_relay)
+                def _():
+                    forward(root, high, high_sem).start()
+
     for root in (roots - 2, roots - 1):
         out_copy(root, root % 2).wait()
 
@@ -126,6 +180,11 @@
         @pl.when(has_low)
         def _():
             down(root).wait_send()
+
+        if rows:
+            @pl.when(root < forwards)
+            def _():
+                forward(root, low, low_sem).wait_send()
 
 
 def on_device(sectors, wave, left_ops, right_ops, deltas, counts):
@@ -144,6 +203,7 @@
             pltpu.VMEM(block, bf16),
             pltpu.VMEM(block, bf16),
             pltpu.VMEM(block, bf16),
+            pltpu.VMEM(block, bf16),
             pltpu.VMEM((slots, width, width), bf16),
             pltpu.VMEM((slots, width, width), bf16),
             pltpu.VMEM((slots * width, width), bf16),
@@ -151,6 +211,8 @@
             pltpu.VMEM((width, slots * width), bf16),
             pltpu.VMEM((2, width, width), bf16),
             pltpu.SemaphoreType.DMA((2, roots)),
+            pltpu.SemaphoreType.DMA((roots,)),
+            pltpu.SemaphoreType.DMA((roots,)),
             pltpu.SemaphoreType.DMA((roots,)),
             pltpu.SemaphoreType.DMA((roots,)),
             pltpu.SemaphoreType.DMA,

time: 55.4 us -> 51 us (0.921)
  the two profiles are of different devices: /device:TPU:9 before, /device:TPU:1 now
where the time goes in v2:
time: 51 us; the launch traced here: 50.8 us
  Pallas kernels  47 us (92%)
  local copies, waits for them, and re-layouts  3.1 us (6%)
  between operations  0.66 us (1%)
    pallas_call x1, Pallas kernels, on_device(): pl.pallas_call(functools.partial(kernel, sectors), out_shape=jax.ShapeDty...  47 us
    unnamed x1, local copies, waits for them, and re-layouts  3.1 us

profile of v2, /device:TPU:1, one launch (start us, length us, event | category | flops | bytes accessed | tf_op | source)
XLA Modules:
  0.0 50.8 jit_solution(13607270164891440442)
XLA Ops:
  0.7 47.0 %shard_map.55 = bf16[16,256,256]{2,1,0:T(8,128)(2,1)} custom-call(s32[1]{0:T(128)S(6)} %copy.7.counts_ref, s32[12]{0:T(128)} %deltas_ref.1, bf16[16,256,256]{2,1,0:T(8,128)(2,1)} %bitcast.3, bf16[12,256,256]{2,1,0:T(8,128)(2,1)} %left_ref.1, bf16[12,256,256]{2,1,0:T(8,128)(2,1)} %right_ref.1), custom_call_target="tpu_custom_call" | custom-call | flops 12884901888 | bytes 7340032 | tf_op jit(solution)/shard_map/pallas_call | solution.py:197
  47.7 3.1 %copy.8 = bf16[1,16,256,256]{3,2,1,0:T(8,128)(2,1)} copy(bf16[1,16,256,256]{3,2,1,0:T(8,128)(2,1)} %bitcast.2) | data formatting | bytes 4194304

commit v3 on v2

--- a/solution.py
+++ b/solution.py
@@ -12,8 +12,8 @@
 
 def kernel(
     sectors, counts_ref, deltas_ref, wave_ref, left_ref, right_ref, out_ref,
-    own, low, high, passing, left, right, right_t, stage, mixed, result,
-    send_sem, low_sem, high_sem, passing_sem, forward_sem, own_sem, op_sem, out_sem,
+    own, low, high, passing, left, right, right_t, stage, mixed, offsets,
+    send_sem, low_sem, high_sem, passing_sem, forward_sem, own_sem, op_sem,
 ):
     roots, width = own.shape[0], own.shape[1]
     slots = left.shape[0]
@@ -51,6 +51,8 @@
     left_copy = pltpu.make_async_copy(left_ref, left, op_sem.at[0])
     right_copy = pltpu.make_async_copy(right_ref, right, op_sem.at[1])
     own_copy = pltpu.make_async_copy(wave_ref, own, own_sem)
+    offsets_copy = pltpu.make_async_copy(deltas_ref, offsets, op_sem.at[2])
+    offsets_copy.start()
     left_copy.start()
     right_copy.start()
     own_copy.start()
@@ -114,6 +116,7 @@
 
     left_copy.wait()
     right_copy.wait()
+    offsets_copy.wait()
     count = counts_ref[0]
 
     @pl.loop(0, slots)
@@ -124,9 +127,6 @@
 
     own_copy.wait()
 
-    def out_copy(root, slot):
-        return pltpu.make_async_copy(result.at[slot], out_ref.at[root], out_sem.at[slot])
-
     @pl.loop(0, roots)
     def _(root):
         @pl.when(has_low)
@@ -141,19 +141,12 @@
         stage[1] = own[root]
         stage[2] = high[root]
         for slot in range(slots):
-            source = stage[deltas_ref[slot] + 1]
+            source = stage[offsets[slot] + 1]
             mixed[:, slot * width:(slot + 1) * width] = jnp.dot(
                 left[slot], source, preferred_element_type=jnp.float32
             ).astype(mixed.dtype)
         total = jnp.dot(mixed[...], right_t[...], preferred_element_type=jnp.float32)
-        now = lax.rem(root, 2)
-
-        @pl.when(root >= 2)
-        def _():
-            out_copy(root - 2, now).wait()
-
-        result[now] = total.astype(result.dtype)
-        out_copy(root, now).start()
+        out_ref[root] = total.astype(out_ref.dtype)
 
         if rows:
             @pl.when(root < forwards)
@@ -168,9 +161,6 @@
                 def _():
                     forward(root, high, high_sem).start()
 
-    for root in (roots - 2, roots - 1):
-        out_copy(root, root % 2).wait()
-
     @pl.loop(0, roots)
     def _(root):
         @pl.when(has_high)
@@ -189,6 +179,10 @@
 
 def on_device(sectors, wave, left_ops, right_ops, deltas, counts):
     wave = wave[0]
+    wave, left_ops, right_ops, deltas = (
+        pltpu.with_memory_space_constraint(x, pltpu.HBM)
+        for x in (wave, left_ops, right_ops, deltas)
+    )
     roots, width = wave.shape[0], wave.shape[1]
     slots = left_ops.shape[0]
     block = (roots, width, width)
@@ -196,9 +190,9 @@
     flops = 4 * roots * slots * width**3
     sigma = pl.pallas_call(
         functools.partial(kernel, sectors),
-        out_shape=jax.ShapeDtypeStruct(block, bf16),
-        in_specs=[pl.BlockSpec(memory_space=pltpu.SMEM)] * 2 + [pl.BlockSpec(memory_space=pl.ANY)] * 3,
-        out_specs=pl.BlockSpec(memory_space=pl.ANY),
+        out_shape=pltpu.VMEM(block, bf16),
+        in_specs=[pl.BlockSpec(memory_space=pltpu.SMEM)] + [pl.BlockSpec(memory_space=pltpu.HBM)] * 4,
+        out_specs=pl.BlockSpec(memory_space=pltpu.VMEM),
         scratch_shapes=[
             pltpu.VMEM(block, bf16),
             pltpu.VMEM(block, bf16),
@@ -209,18 +203,17 @@
             pltpu.VMEM((slots * width, width), bf16),
             pltpu.VMEM((3, width, width), bf16),
             pltpu.VMEM((width, slots * width), bf16),
-            pltpu.VMEM((2, width, width), bf16),
+            pltpu.SMEM(deltas.shape, deltas.dtype),
             pltpu.SemaphoreType.DMA((2, roots)),
             pltpu.SemaphoreType.DMA((roots,)),
             pltpu.SemaphoreType.DMA((roots,)),
             pltpu.SemaphoreType.DMA((roots,)),
             pltpu.SemaphoreType.DMA((roots,)),
             pltpu.SemaphoreType.DMA,
-            pltpu.SemaphoreType.DMA((2,)),
-            pltpu.SemaphoreType.DMA((2,)),
+            pltpu.SemaphoreType.DMA((3,)),
         ],
         compiler_params=pltpu.CompilerParams(
-            collective_id=0, has_side_effects=True, vmem_limit_bytes=60 * 2**20
+            collective_id=0, has_side_effects=True, vmem_limit_bytes=48 * 2**20
         ),
         cost_estimate=pl.CostEstimate(flops=flops, bytes_accessed=7 * 2**20, transcendentals=0),
     )(counts, deltas, wave, left_ops, right_ops)

time: 51 us -> 47.9 us (0.939)
  local copies, waits for them, and re-layouts: 3.1 us -> 1.32 us
  Pallas kernels: 47 us -> 45.8 us
    unnamed x1, local copies, waits for them, and re-layouts: 3.1 us -> 1.32 us
    pallas_call x1, Pallas kernels: 47 us -> 45.8 us  [on_device(): pl.pallas_call(functools.partial(kernel, sectors), out_shape=pltpu.VMEM(b...]
where the time goes in v3:
time: 47.9 us; the launch traced here: 47.8 us
  Pallas kernels  45.8 us (96%)
  local copies, waits for them, and re-layouts  1.32 us (3%)
  between operations  0.66 us (1%)
    pallas_call x1, Pallas kernels, on_device(): pl.pallas_call(functools.partial(kernel, sectors), out_shape=pltpu.VMEM(b...  45.8 us
    unnamed x1, local copies, waits for them, and re-layouts  1.32 us

profile of v3, /device:TPU:1, one launch (start us, length us, event | category | flops | bytes accessed | tf_op | source)
XLA Modules:
  0.0 47.8 jit_solution(155543934914153585)
XLA Ops:
  0.7 45.8 %shard_map.55 = bf16[16,256,256]{2,1,0:T(8,128)(2,1)S(1)} custom-call(s32[1]{0:T(128)S(6)} %copy.8.counts_ref, s32[12]{0:T(128)} %deltas_ref.1, bf16[16,256,256]{2,1,0:T(8,128)(2,1)} %bitcast.3, bf16[12,256,256]{2,1,0:T(8,128)(2,1)} %left_ref.1, bf16[12,256,256]{2,1,0:T(8,128)(2,1)} %right_ref.1), custom_call_target="tpu_custom_call" | custom-call | flops 12884901888 | bytes 7340032 | tf_op jit(solution)/shard_map/pallas_call | solution.py:191
  46.5 1.3 %copy.7 = bf16[1,16,256,256]{3,2,1,0:T(8,128)(2,1)} copy(bf16[1,16,256,256]{3,2,1,0:T(8,128)(2,1)S(1)} %bitcast.2) | data formatting | bytes 4194304

commit v4 on v3

--- a/solution.py
+++ b/solution.py
@@ -10,9 +10,33 @@
 MESH = pl.DeviceIdType.MESH
 
 
+def apply_root(stage, offsets, left, right_t, mixed):
+    slots, width = left.shape[0], left.shape[1]
+    for slot in range(slots):
+        source = stage[offsets[slot] + 1]
+        mixed[:, slot * width:(slot + 1) * width] = jnp.dot(
+            left[slot], source, preferred_element_type=jnp.float32
+        ).astype(mixed.dtype)
+    return jnp.dot(mixed[...], right_t[...], preferred_element_type=jnp.float32)
+
+
+def finish(offsets, stage, left, right_t, done_ref, out_ref, mixed, result, done_sem, last_sem):
+    last = out_ref.shape[0] - 1
+    done_copy = pltpu.make_async_copy(
+        done_ref.at[pl.ds(0, last)], out_ref.at[pl.ds(0, last)], done_sem
+    )
+    done_copy.start()
+    result[...] = apply_root(stage, offsets, left, right_t, mixed).astype(result.dtype)
+    last_copy = pltpu.make_async_copy(result, out_ref.at[last], last_sem)
+    last_copy.start()
+    done_copy.wait()
+    last_copy.wait()
+
+
 def kernel(
-    sectors, counts_ref, deltas_ref, wave_ref, left_ref, right_ref, out_ref,
-    own, low, high, passing, left, right, right_t, stage, mixed, offsets,
+    sectors, counts_ref, deltas_ref, wave_ref, left_ref, right_ref,
+    out_ref, left, right_t, stage, offsets,
+    own, low, high, passing, right, mixed,
     send_sem, low_sem, high_sem, passing_sem, forward_sem, own_sem, op_sem,
 ):
     roots, width = own.shape[0], own.shape[1]
@@ -127,8 +151,7 @@
 
     own_copy.wait()
 
-    @pl.loop(0, roots)
-    def _(root):
+    def gather(root):
         @pl.when(has_low)
         def _():
             up(root).wait_recv()
@@ -140,12 +163,25 @@
         stage[0] = low[root]
         stage[1] = own[root]
         stage[2] = high[root]
-        for slot in range(slots):
-            source = stage[offsets[slot] + 1]
-            mixed[:, slot * width:(slot + 1) * width] = jnp.dot(
-                left[slot], source, preferred_element_type=jnp.float32
-            ).astype(mixed.dtype)
-        total = jnp.dot(mixed[...], right_t[...], preferred_element_type=jnp.float32)
+
+    def settle(root):
+        @pl.when(has_high)
+        def _():
+            up(root).wait_send()
+
+        @pl.when(has_low)
+        def _():
+            down(root).wait_send()
+
+        if rows:
+            @pl.when(root < forwards)
+            def _():
+                forward(root, low, low_sem).wait_send()
+
+    @pl.loop(0, roots - 1)
+    def _(root):
+        gather(root)
+        total = apply_root(stage, offsets, left, right_t, mixed)
         out_ref[root] = total.astype(out_ref.dtype)
 
         if rows:
@@ -161,20 +197,15 @@
                 def _():
                     forward(root, high, high_sem).start()
 
-    @pl.loop(0, roots)
+        @pl.when(root >= 4)
+        def _():
+            settle(root - 4)
+
+    gather(roots - 1)
+
+    @pl.loop(roots - 5, roots)
     def _(root):
-        @pl.when(has_high)
-        def _():
-            up(root).wait_send()
-
-        @pl.when(has_low)
-        def _():
-            down(root).wait_send()
-
-        if rows:
-            @pl.when(root < forwards)
-            def _():
-                forward(root, low, low_sem).wait_send()
+        settle(root)
 
 
 def on_device(sectors, wave, left_ops, right_ops, deltas, counts):
@@ -188,22 +219,28 @@
     block = (roots, width, width)
     bf16 = wave.dtype
     flops = 4 * roots * slots * width**3
-    sigma = pl.pallas_call(
+    operand = (slots, width, width)
+    operand_cat = (slots * width, width)
+    held = pl.BlockSpec(memory_space=pltpu.VMEM)
+    scalars = pl.BlockSpec(memory_space=pltpu.SMEM)
+    done, left, right_t, stage, offsets = pl.pallas_call(
         functools.partial(kernel, sectors),
-        out_shape=pltpu.VMEM(block, bf16),
-        in_specs=[pl.BlockSpec(memory_space=pltpu.SMEM)] + [pl.BlockSpec(memory_space=pltpu.HBM)] * 4,
-        out_specs=pl.BlockSpec(memory_space=pltpu.VMEM),
+        out_shape=(
+            pltpu.VMEM(block, bf16),
+            pltpu.VMEM(operand, bf16),
+            pltpu.VMEM(operand_cat, bf16),
+            pltpu.VMEM((3, width, width), bf16),
+            pltpu.SMEM(deltas.shape, deltas.dtype),
+        ),
+        in_specs=[scalars] + [pl.BlockSpec(memory_space=pltpu.HBM)] * 4,
+        out_specs=(held, held, held, held, scalars),
         scratch_shapes=[
             pltpu.VMEM(block, bf16),
             pltpu.VMEM(block, bf16),
             pltpu.VMEM(block, bf16),
             pltpu.VMEM(block, bf16),
-            pltpu.VMEM((slots, width, width), bf16),
-            pltpu.VMEM((slots, width, width), bf16),
-            pltpu.VMEM((slots * width, width), bf16),
-            pltpu.VMEM((3, width, width), bf16),
+            pltpu.VMEM(operand, bf16),
             pltpu.VMEM((width, slots * width), bf16),
-            pltpu.SMEM(deltas.shape, deltas.dtype),
             pltpu.SemaphoreType.DMA((2, roots)),
             pltpu.SemaphoreType.DMA((roots,)),
             pltpu.SemaphoreType.DMA((roots,)),
@@ -217,6 +254,22 @@
         ),
         cost_estimate=pl.CostEstimate(flops=flops, bytes_accessed=7 * 2**20, transcendentals=0),
     )(counts, deltas, wave, left_ops, right_ops)
+    sigma = pl.pallas_call(
+        finish,
+        out_shape=jax.ShapeDtypeStruct(block, bf16),
+        in_specs=[scalars] + [held] * 4,
+        out_specs=pl.BlockSpec(memory_space=pl.ANY),
+        scratch_shapes=[
+            pltpu.VMEM((width, slots * width), bf16),
+            pltpu.VMEM((width, width), bf16),
+            pltpu.SemaphoreType.DMA,
+            pltpu.SemaphoreType.DMA,
+        ],
+        compiler_params=pltpu.CompilerParams(vmem_limit_bytes=48 * 2**20),
+        cost_estimate=pl.CostEstimate(
+            flops=flops // roots, bytes_accessed=2 * 2**20, transcendentals=0
+        ),
+    )(offsets, stage, left, right_t, done)
     return sigma[None]
 
 

time: 47.9 us -> 47.4 us (0.990)
  local copies, waits for them, and re-layouts: 1.32 us -> 0 us
  Pallas kernels: 45.8 us -> 46.6 us
    unnamed x1 -> x0, local copies, waits for them, and re-layouts: 1.32 us -> none
    pallas_call x1 -> x2, Pallas kernels: 45.8 us -> 46.6 us  [the longest x1 44.5 us: on_device(): pl.pallas_call(functools.partial(kernel, sectors), out_shape=(pltpu.VMEM(...]
where the time goes in v4:
time: 47.4 us; the launch traced here: 47.2 us
  Pallas kernels  46.6 us (98%)
  between operations  0.66 us (1%)
    pallas_call x1, Pallas kernels, on_device(): pl.pallas_call(functools.partial(kernel, sectors), out_shape=(pltpu.VMEM(...  44.5 us
    pallas_call x1, Pallas kernels, on_device(): pl.pallas_call(finish, out_shape=jax.ShapeDtypeStruct(block, bf16), in_sp...  2.06 us

profile of v4, /device:TPU:1, one launch (start us, length us, event | category | flops | bytes accessed | tf_op | source)
XLA Modules:
  0.0 47.2 jit_solution(13535592339464983458)
XLA Ops:
  0.7 44.5 %shard_map.55 = (bf16[16,256,256]{2,1,0:T(8,128)(2,1)S(1)}, bf16[12,256,256]{2,1,0:T(8,128)(2,1)S(1)}, bf16[3072,256]{1,0:T(8,128)(2,1)S(1)}, bf16[3,256,256]{2,1,0:T(8,128)(2,1)S(1)}, s32[12]{0:T(128)S(4)}) custom-call(s32[1]{0:T(128)S(6)} %copy.6.counts_ref, s32[12]{0:T(128)} %deltas_ref.1, bf16[16,256,256]{2,1,0:T(8,128)(2,1)} %bitcast.2, ...), custom_call_target="tpu_custom_call" | custom-call | flops 12884901888 | bytes 7340032 | tf_op jit(solution)/shard_map/pallas_call | solution.py:226
  45.2 2.1 %shard_map.56 = bf16[16,256,256]{2,1,0:T(8,128)(2,1)} custom-call(s32[12]{0:T(128)S(4)} %get-tuple-element.10.offsets, bf16[3,256,256]{2,1,0:T(8,128)(2,1)S(1)} %get-tuple-element.11.stage, bf16[12,256,256]{2,1,0:T(8,128)(2,1)S(1)} %get-tuple-element.12.left, bf16[3072,256]{1,0:T(8,128)(2,1)S(1)} %get-tuple-element.13.right_t, ...), custom_call_target="tpu_custom_call" | custom-call | flops 805306368 | bytes 2097152 | tf_op jit(solution)/shard_map/pallas_call | solution.py:257

commit v5 on v4

--- a/solution.py
+++ b/solution.py
@@ -12,12 +12,18 @@
 
 def apply_root(stage, offsets, left, right_t, mixed):
     slots, width = left.shape[0], left.shape[1]
-    for slot in range(slots):
-        source = stage[offsets[slot] + 1]
-        mixed[:, slot * width:(slot + 1) * width] = jnp.dot(
-            left[slot], source, preferred_element_type=jnp.float32
-        ).astype(mixed.dtype)
-    return jnp.dot(mixed[...], right_t[...], preferred_element_type=jnp.float32)
+    group = 3 if slots % 3 == 0 else 1
+    total = None
+    for first in range(0, slots, group):
+        for slot in range(first, first + group):
+            source = stage[offsets[slot] + 1]
+            mixed[:, slot * width:(slot + 1) * width] = jnp.dot(
+                left[slot], source, preferred_element_type=jnp.float32
+            ).astype(mixed.dtype)
+        span = slice(first * width, (first + group) * width)
+        part = jnp.dot(mixed[:, span], right_t[span, :], preferred_element_type=jnp.float32)
+        total = part if total is None else total + part
+    return total
 
 
 def finish(offsets, stage, left, right_t, done_ref, out_ref, mixed, result, done_sem, last_sem):

time: 47.4 us -> 47.3 us (level)
  no operation moved by 1% of the time
where the time goes in v5:
time: 47.3 us; the launch traced here: 47.2 us
  Pallas kernels  46.5 us (98%)
  between operations  0.66 us (1%)
    pallas_call x1, Pallas kernels, on_device(): pl.pallas_call(functools.partial(kernel, sectors), out_shape=(pltpu.VMEM(...  44.5 us
    pallas_call x1, Pallas kernels, on_device(): pl.pallas_call(finish, out_shape=jax.ShapeDtypeStruct(block, bf16), in_sp...  1.97 us

profile of v5, /device:TPU:1, one launch (start us, length us, event | category | flops | bytes accessed | tf_op | source)
XLA Modules:
  0.0 47.2 jit_solution(9240404811471285283)
XLA Ops:
  0.7 44.5 %shard_map.55 = (bf16[16,256,256]{2,1,0:T(8,128)(2,1)S(1)}, bf16[12,256,256]{2,1,0:T(8,128)(2,1)S(1)}, bf16[3072,256]{1,0:T(8,128)(2,1)S(1)}, bf16[3,256,256]{2,1,0:T(8,128)(2,1)S(1)}, s32[12]{0:T(128)S(4)}) custom-call(s32[1]{0:T(128)S(6)} %copy.6.counts_ref, s32[12]{0:T(128)} %deltas_ref.1, bf16[16,256,256]{2,1,0:T(8,128)(2,1)} %bitcast.2, ...), custom_call_target="tpu_custom_call" | custom-call | flops 12884901888 | bytes 7340032 | tf_op jit(solution)/shard_map/pallas_call | solution.py:232
  45.2 2.0 %shard_map.56 = bf16[16,256,256]{2,1,0:T(8,128)(2,1)} custom-call(s32[12]{0:T(128)S(4)} %get-tuple-element.10.offsets, bf16[3,256,256]{2,1,0:T(8,128)(2,1)S(1)} %get-tuple-element.11.stage, bf16[12,256,256]{2,1,0:T(8,128)(2,1)S(1)} %get-tuple-element.12.left, bf16[3072,256]{1,0:T(8,128)(2,1)S(1)} %get-tuple-element.13.right_t, ...), custom_call_target="tpu_custom_call" | custom-call | flops 805306368 | bytes 2097152 | tf_op jit(solution)/shard_map/pallas_call | solution.py:263

commit v6 on v4

--- a/solution.py
+++ b/solution.py
@@ -76,59 +76,69 @@
     right_copy = pltpu.make_async_copy(right_ref, right, op_sem.at[1])
     own_copy = pltpu.make_async_copy(wave_ref, own, own_sem)
     offsets_copy = pltpu.make_async_copy(deltas_ref, offsets, op_sem.at[2])
+    pl.semaphore_wait(barrier, sum(present.astype(jnp.int32) for present, _ in partners))
+
+    def up(root):
+        return pltpu.make_async_remote_copy(
+            src_ref=wave_ref.at[root], dst_ref=low.at[root],
+            send_sem=send_sem.at[0, root], recv_sem=low_sem.at[root],
+            device_id={"sector": me + 1}, device_id_type=MESH,
+        )
+
+    def down(root):
+        return pltpu.make_async_remote_copy(
+            src_ref=wave_ref.at[root], dst_ref=high.at[root],
+            send_sem=send_sem.at[1, root], recv_sem=high_sem.at[root],
+            device_id={"sector": me - 1}, device_id_type=MESH,
+        )
+
+    def aside(root, step, way, corner):
+        return pltpu.make_async_remote_copy(
+            src_ref=wave_ref.at[root], dst_ref=passing.at[step],
+            send_sem=send_sem.at[way, root], recv_sem=passing_sem.at[step],
+            device_id={"sector": corner}, device_id_type=MESH,
+        )
+
+    def forward(step, target, target_sem):
+        root = roots - forwards + step
+        return pltpu.make_async_remote_copy(
+            src_ref=passing.at[step], dst_ref=target.at[root],
+            send_sem=forward_sem.at[step], recv_sem=target_sem.at[root],
+            device_id={"sector": ahead}, device_id_type=MESH,
+        )
+
+    def send(step):
+        @pl.when(jnp.logical_and(has_high, step < roots - up_detour))
+        def _():
+            up(step).start()
+
+        @pl.when(jnp.logical_and(has_low, step < roots - down_detour))
+        def _():
+            down(step).start()
+
+        if rows:
+            @pl.when(step < up_detour)
+            def _():
+                aside(roots - up_detour + step, step, 0, me - 2).start()
+
+            @pl.when(step < down_detour)
+            def _():
+                aside(roots - down_detour + step, step, 1, me + 2).start()
+
+    lead = 2
+
+    @pl.loop(0, lead)
+    def _(step):
+        send(step)
+
     offsets_copy.start()
     left_copy.start()
     right_copy.start()
     own_copy.start()
-    pl.semaphore_wait(barrier, sum(present.astype(jnp.int32) for present, _ in partners))
-
-    def up(root):
-        return pltpu.make_async_remote_copy(
-            src_ref=wave_ref.at[root], dst_ref=low.at[root],
-            send_sem=send_sem.at[0, root], recv_sem=low_sem.at[root],
-            device_id={"sector": me + 1}, device_id_type=MESH,
-        )
-
-    def down(root):
-        return pltpu.make_async_remote_copy(
-            src_ref=wave_ref.at[root], dst_ref=high.at[root],
-            send_sem=send_sem.at[1, root], recv_sem=high_sem.at[root],
-            device_id={"sector": me - 1}, device_id_type=MESH,
-        )
-
-    def aside(root, step, way, corner):
-        return pltpu.make_async_remote_copy(
-            src_ref=wave_ref.at[root], dst_ref=passing.at[step],
-            send_sem=send_sem.at[way, root], recv_sem=passing_sem.at[step],
-            device_id={"sector": corner}, device_id_type=MESH,
-        )
-
-    def forward(step, target, target_sem):
-        root = roots - forwards + step
-        return pltpu.make_async_remote_copy(
-            src_ref=passing.at[step], dst_ref=target.at[root],
-            send_sem=forward_sem.at[step], recv_sem=target_sem.at[root],
-            device_id={"sector": ahead}, device_id_type=MESH,
-        )
-
-    @pl.loop(0, roots)
+
+    @pl.loop(lead, roots)
     def _(step):
-        @pl.when(jnp.logical_and(has_high, step < roots - up_detour))
-        def _():
-            up(step).start()
-
-        @pl.when(jnp.logical_and(has_low, step < roots - down_detour))
-        def _():
-            down(step).start()
-
-        if rows:
-            @pl.when(step < up_detour)
-            def _():
-                aside(roots - up_detour + step, step, 0, me - 2).start()
-
-            @pl.when(step < down_detour)
-            def _():
-                aside(roots - down_detour + step, step, 1, me + 2).start()
+        send(step)
 
     @pl.when(jnp.logical_not(has_low))
     def _():

time: 47.4 us -> 47.4 us (level)
  no operation moved by 1% of the time
where the time goes in v6:
time: 47.4 us; the launch traced here: 47.2 us
  Pallas kernels  46.6 us (98%)
  between operations  0.66 us (1%)
    pallas_call x1, Pallas kernels, on_device(): pl.pallas_call(functools.partial(kernel, sectors), out_shape=(pltpu.VMEM(...  44.5 us
    pallas_call x1, Pallas kernels, on_device(): pl.pallas_call(finish, out_shape=jax.ShapeDtypeStruct(block, bf16), in_sp...  2.06 us

profile of v6, /device:TPU:1, one launch (start us, length us, event | category | flops | bytes accessed | tf_op | source)
XLA Modules:
  0.0 47.2 jit_solution(15480964073088075561)
XLA Ops:
  0.7 44.5 %shard_map.55 = (bf16[16,256,256]{2,1,0:T(8,128)(2,1)S(1)}, bf16[12,256,256]{2,1,0:T(8,128)(2,1)S(1)}, bf16[3072,256]{1,0:T(8,128)(2,1)S(1)}, bf16[3,256,256]{2,1,0:T(8,128)(2,1)S(1)}, s32[12]{0:T(128)S(4)}) custom-call(s32[1]{0:T(128)S(6)} %copy.6.counts_ref, s32[12]{0:T(128)} %deltas_ref.1, bf16[16,256,256]{2,1,0:T(8,128)(2,1)} %bitcast.2, ...), custom_call_target="tpu_custom_call" | custom-call | flops 12884901888 | bytes 7340032 | tf_op jit(solution)/shard_map/pallas_call | solution.py:236
  45.2 2.1 %shard_map.56 = bf16[16,256,256]{2,1,0:T(8,128)(2,1)} custom-call(s32[12]{0:T(128)S(4)} %get-tuple-element.10.offsets, bf16[3,256,256]{2,1,0:T(8,128)(2,1)S(1)} %get-tuple-element.11.stage, bf16[12,256,256]{2,1,0:T(8,128)(2,1)S(1)} %get-tuple-element.12.left, bf16[3072,256]{1,0:T(8,128)(2,1)S(1)} %get-tuple-element.13.right_t, ...), custom_call_target="tpu_custom_call" | custom-call | flops 805306368 | bytes 2097152 | tf_op jit(solution)/shard_map/pallas_call | solution.py:267

commit v7 on v4

--- a/solution.py
+++ b/solution.py
@@ -11,7 +11,8 @@
 
 
 def apply_root(stage, offsets, left, right_t, mixed):
-    slots, width = left.shape[0], left.shape[1]
+    width = left.shape[1]
+    slots = right_t.shape[0] // width
     for slot in range(slots):
         source = stage[offsets[slot] + 1]
         mixed[:, slot * width:(slot + 1) * width] = jnp.dot(
@@ -20,13 +21,45 @@
     return jnp.dot(mixed[...], right_t[...], preferred_element_type=jnp.float32)
 
 
-def finish(offsets, stage, left, right_t, done_ref, out_ref, mixed, result, done_sem, last_sem):
+def finish(
+    reads, late, left, right_t, partial, done_ref, out_ref,
+    order, mixed, total, result, done_sem, last_sem,
+):
     last = out_ref.shape[0] - 1
+    width = left.shape[1]
+    slots = left.shape[0] - 1
+    group = mixed.shape[1] // width
     done_copy = pltpu.make_async_copy(
         done_ref.at[pl.ds(0, last)], out_ref.at[pl.ds(0, last)], done_sem
     )
     done_copy.start()
-    result[...] = apply_root(stage, offsets, left, right_t, mixed).astype(result.dtype)
+
+    for place in range(slots + group):
+        order[place] = slots
+    found = jnp.int32(0)
+    for slot in range(slots):
+        order[found] = jnp.where(reads[slot] == 1, slot, slots)
+        found = found + reads[slot]
+    total[...] = partial[...]
+
+    def add_group(step, carry):
+        parts = None
+        for place in range(group):
+            slot = order[step * group + place]
+            span = slice(place * width, (place + 1) * width)
+            mixed[:, span] = jnp.dot(
+                left[slot], late[...], preferred_element_type=jnp.float32
+            ).astype(mixed.dtype)
+            row = pl.multiple_of(jnp.minimum(slot, slots - 1) * width, width)
+            part = jnp.dot(
+                mixed[:, span], right_t[pl.ds(row, width), :], preferred_element_type=jnp.float32
+            )
+            parts = part if parts is None else parts + part
+        total[...] += parts
+        return carry
+
+    lax.fori_loop(0, lax.div(found + group - 1, group), add_group, 0)
+    result[...] = total[...].astype(result.dtype)
     last_copy = pltpu.make_async_copy(result, out_ref.at[last], last_sem)
     last_copy.start()
     done_copy.wait()
@@ -35,14 +68,16 @@
 
 def kernel(
     sectors, counts_ref, deltas_ref, wave_ref, left_ref, right_ref,
-    out_ref, left, right_t, stage, offsets,
-    own, low, high, passing, right, mixed,
+    out_ref, left, right_t, late, partial, reads,
+    own, low, high, passing, right, mixed, stage, offsets,
     send_sem, low_sem, high_sem, passing_sem, forward_sem, own_sem, op_sem,
 ):
     roots, width = own.shape[0], own.shape[1]
-    slots = left.shape[0]
+    slots = right.shape[0]
+    last = roots - 1
     me = lax.axis_index("sector")
     has_low, has_high = me > 0, me < sectors - 1
+    odd = lax.rem(me, 2) == 1
 
     rows = sectors // 4 if sectors == 16 else 0
     row, place = lax.div(me, 4), lax.rem(me, 4)
@@ -72,7 +107,7 @@
         def _(partner=partner):
             pl.semaphore_signal(barrier, inc=1, device_id={"sector": partner}, device_id_type=MESH)
 
-    left_copy = pltpu.make_async_copy(left_ref, left, op_sem.at[0])
+    left_copy = pltpu.make_async_copy(left_ref, left.at[pl.ds(0, slots)], op_sem.at[0])
     right_copy = pltpu.make_async_copy(right_ref, right, op_sem.at[1])
     own_copy = pltpu.make_async_copy(wave_ref, own, own_sem)
     offsets_copy = pltpu.make_async_copy(deltas_ref, offsets, op_sem.at[2])
@@ -115,11 +150,11 @@
     def _(step):
         @pl.when(jnp.logical_and(has_high, step < roots - up_detour))
         def _():
-            up(step).start()
+            up(jnp.where(odd, step, lax.rem(step + last, roots))).start()
 
         @pl.when(jnp.logical_and(has_low, step < roots - down_detour))
         def _():
-            down(step).start()
+            down(jnp.where(odd, lax.rem(step + last, roots), step)).start()
 
         if rows:
             @pl.when(step < up_detour)
@@ -142,10 +177,15 @@
     right_copy.wait()
     offsets_copy.wait()
     count = counts_ref[0]
+    far = jnp.where(odd, 1, -1)
+    left[slots] = jnp.zeros((width, width), left.dtype)
 
     @pl.loop(0, slots)
     def _(slot):
         live = jnp.where(slot < count, 1.0, 0.0).astype(jnp.float32)
+        reads[slot] = jnp.where(
+            jnp.logical_and(slot < count, offsets[slot] == far), 1, 0
+        ).astype(jnp.int32)
         left[slot] = (left[slot].astype(jnp.float32) * live).astype(left.dtype)
         right_t[pl.ds(pl.multiple_of(slot * width, width), width), :] = right[slot].T
 
@@ -178,7 +218,22 @@
             def _():
                 forward(root, low, low_sem).wait_send()
 
-    @pl.loop(0, roots - 1)
+    @pl.when(odd)
+    def _():
+        up(last).wait_recv()
+        stage[0] = low[last]
+        stage[2] = jnp.zeros((width, width), stage.dtype)
+
+    @pl.when(jnp.logical_not(odd))
+    def _():
+        down(last).wait_recv()
+        stage[0] = jnp.zeros((width, width), stage.dtype)
+        stage[2] = high[last]
+
+    stage[1] = own[last]
+    partial[...] = apply_root(stage, offsets, left, right_t, mixed)
+
+    @pl.loop(0, last)
     def _(root):
         gather(root)
         total = apply_root(stage, offsets, left, right_t, mixed)
@@ -201,7 +256,21 @@
         def _():
             settle(root - 4)
 
-    gather(roots - 1)
+    @pl.when(odd)
+    def _():
+        @pl.when(has_high)
+        def _():
+            down(last).wait_recv()
+
+        late[...] = high[last]
+
+    @pl.when(jnp.logical_not(odd))
+    def _():
+        @pl.when(has_low)
+        def _():
+            up(last).wait_recv()
+
+        late[...] = low[last]
 
     @pl.loop(roots - 5, roots)
     def _(root):
@@ -223,17 +292,18 @@
     operand_cat = (slots * width, width)
     held = pl.BlockSpec(memory_space=pltpu.VMEM)
     scalars = pl.BlockSpec(memory_space=pltpu.SMEM)
-    done, left, right_t, stage, offsets = pl.pallas_call(
+    done, left, right_t, late, partial, reads = pl.pallas_call(
         functools.partial(kernel, sectors),
         out_shape=(
             pltpu.VMEM(block, bf16),
-            pltpu.VMEM(operand, bf16),
+            pltpu.VMEM((slots + 1, width, width), bf16),
             pltpu.VMEM(operand_cat, bf16),
-            pltpu.VMEM((3, width, width), bf16),
+            pltpu.VMEM((width, width), bf16),
+            pltpu.VMEM((width, width), jnp.float32),
             pltpu.SMEM(deltas.shape, deltas.dtype),
         ),
         in_specs=[scalars] + [pl.BlockSpec(memory_space=pltpu.HBM)] * 4,
-        out_specs=(held, held, held, held, scalars),
+        out_specs=(held, held, held, held, held, scalars),
         scratch_shapes=[
             pltpu.VMEM(block, bf16),
             pltpu.VMEM(block, bf16),
@@ -241,6 +311,8 @@
             pltpu.VMEM(block, bf16),
             pltpu.VMEM(operand, bf16),
             pltpu.VMEM((width, slots * width), bf16),
+            pltpu.VMEM((3, width, width), bf16),
+            pltpu.SMEM(deltas.shape, deltas.dtype),
             pltpu.SemaphoreType.DMA((2, roots)),
             pltpu.SemaphoreType.DMA((roots,)),
             pltpu.SemaphoreType.DMA((roots,)),
@@ -257,10 +329,12 @@
     sigma = pl.pallas_call(
         finish,
         out_shape=jax.ShapeDtypeStruct(block, bf16),
-        in_specs=[scalars] + [held] * 4,
+        in_specs=[scalars] + [held] * 5,
         out_specs=pl.BlockSpec(memory_space=pl.ANY),
         scratch_shapes=[
-            pltpu.VMEM((width, slots * width), bf16),
+            pltpu.SMEM((slots + 3,), jnp.int32),
+            pltpu.VMEM((width, 3 * width), bf16),
+            pltpu.VMEM((width, width), jnp.float32),
             pltpu.VMEM((width, width), bf16),
             pltpu.SemaphoreType.DMA,
             pltpu.SemaphoreType.DMA,
@@ -269,7 +343,7 @@
         cost_estimate=pl.CostEstimate(
             flops=flops // roots, bytes_accessed=2 * 2**20, transcendentals=0
         ),
-    )(offsets, stage, left, right_t, done)
+    )(reads, late, left, right_t, partial, done)
     return sigma[None]
 
 

time: 47.4 us -> 46.8 us (0.987)
  Pallas kernels: 46.6 us -> 45.8 us
    pallas_call x1, Pallas kernels: 2.06 us -> 1.32 us  [on_device(): pl.pallas_call(finish, out_shape=jax.ShapeDtypeStruct(block, bf16), in_sp...]
where the time goes in v7:
time: 46.8 us; the launch traced here: 46.5 us
  Pallas kernels  45.8 us (98%)
  between operations  0.66 us (1%)
    pallas_call x1, Pallas kernels, on_device(): pl.pallas_call(functools.partial(kernel, sectors), out_shape=(pltpu.VMEM(...  44.5 us
    pallas_call x1, Pallas kernels, on_device(): pl.pallas_call(finish, out_shape=jax.ShapeDtypeStruct(block, bf16), in_sp...  1.32 us

profile of v7, /device:TPU:1, one launch (start us, length us, event | category | flops | bytes accessed | tf_op | source)
XLA Modules:
  0.0 46.5 jit_solution(14044742164461857417)
XLA Ops:
  0.7 44.5 %shard_map.55 = (bf16[16,256,256]{2,1,0:T(8,128)(2,1)S(1)}, bf16[13,256,256]{2,1,0:T(8,128)(2,1)S(1)}, bf16[3072,256]{1,0:T(8,128)(2,1)S(1)}, bf16[256,256]{1,0:...) custom-call(s32[1]{0:T(128)S(6)} %copy.6.counts_ref, s32[12]{0:T(128)} %deltas_ref.1, ...), custom_call_target="tpu_custom_call" | custom-call | flops 12884901888 | bytes 7340032 | tf_op jit(solution)/shard_map/pallas_call | solution.py:295
  45.2 1.3 %shard_map.56 = bf16[16,256,256]{2,1,0:T(8,128)(2,1)} custom-call(s32[12]{0:T(128)S(4)} %get-tuple-element.11.reads, bf16[256,256]{1,0:T(8,128)(2,1)S(1)} %get-tuple-element.12.late, bf16[13,256,256]{2,1,0:T(8,128)(2,1)S(1)} %get-tuple-element.13.left, bf16[3072,256]{1,0:T(8,128)(2,1)S(1)} %get-tuple-element.14.right_t, ...), custom_call_target="tpu_custom_call" | custom-call | flops 805306368 | bytes 2097152 | tf_op jit(solution)/shard_map/pallas_call | solution.py:329

commit v8 on v7

--- a/solution.py
+++ b/solution.py
@@ -23,43 +23,44 @@
 
 def finish(
     reads, late, left, right_t, partial, done_ref, out_ref,
-    order, mixed, total, result, done_sem, last_sem,
+    order, mixed, right, result, done_sem, last_sem,
 ):
     last = out_ref.shape[0] - 1
     width = left.shape[1]
     slots = left.shape[0] - 1
-    group = mixed.shape[1] // width
     done_copy = pltpu.make_async_copy(
         done_ref.at[pl.ds(0, last)], out_ref.at[pl.ds(0, last)], done_sem
     )
     done_copy.start()
 
-    for place in range(slots + group):
+    for place in range(slots):
         order[place] = slots
     found = jnp.int32(0)
     for slot in range(slots):
         order[found] = jnp.where(reads[slot] == 1, slot, slots)
         found = found + reads[slot]
-    total[...] = partial[...]
-
-    def add_group(step, carry):
-        parts = None
-        for place in range(group):
-            slot = order[step * group + place]
+
+    def add_late(size):
+        for place in range(size):
+            slot = order[place]
             span = slice(place * width, (place + 1) * width)
+            row = pl.multiple_of(jnp.minimum(slot, slots - 1) * width, width)
+            right[span, :] = right_t[pl.ds(row, width), :]
             mixed[:, span] = jnp.dot(
                 left[slot], late[...], preferred_element_type=jnp.float32
             ).astype(mixed.dtype)
-            row = pl.multiple_of(jnp.minimum(slot, slots - 1) * width, width)
-            part = jnp.dot(
-                mixed[:, span], right_t[pl.ds(row, width), :], preferred_element_type=jnp.float32
-            )
-            parts = part if parts is None else parts + part
-        total[...] += parts
-        return carry
-
-    lax.fori_loop(0, lax.div(found + group - 1, group), add_group, 0)
-    result[...] = total[...].astype(result.dtype)
+        depth = slice(0, size * width)
+        added = jnp.dot(mixed[:, depth], right[depth, :], preferred_element_type=jnp.float32)
+        result[...] = (partial[...] + added).astype(result.dtype)
+
+    below = -1
+    for size in sorted({-(-slots // 3), -(-2 * slots // 3), slots}):
+        @pl.when(jnp.logical_and(found > below, found <= size))
+        def _(size=size):
+            add_late(size)
+
+        below = size
+
     last_copy = pltpu.make_async_copy(result, out_ref.at[last], last_sem)
     last_copy.start()
     done_copy.wait()
@@ -332,9 +333,9 @@
         in_specs=[scalars] + [held] * 5,
         out_specs=pl.BlockSpec(memory_space=pl.ANY),
         scratch_shapes=[
-            pltpu.SMEM((slots + 3,), jnp.int32),
-            pltpu.VMEM((width, 3 * width), bf16),
-            pltpu.VMEM((width, width), jnp.float32),
+            pltpu.SMEM((slots,), jnp.int32),
+            pltpu.VMEM((width, slots * width), bf16),
+            pltpu.VMEM((slots * width, width), bf16),
             pltpu.VMEM((width, width), bf16),
             pltpu.SemaphoreType.DMA,
             pltpu.SemaphoreType.DMA,

time: 46.8 us -> 46.6 us (level)
  no operation moved by 1% of the time
where the time goes in v8:
time: 46.6 us; the launch traced here: 46.5 us
  Pallas kernels  45.8 us (98%)
  between operations  0.66 us (1%)
    pallas_call x1, Pallas kernels, on_device(): pl.pallas_call(functools.partial(kernel, sectors), out_shape=(pltpu.VMEM(...  44.5 us
    pallas_call x1, Pallas kernels, on_device(): pl.pallas_call(finish, out_shape=jax.ShapeDtypeStruct(block, bf16), in_sp...  1.32 us

profile of v8, /device:TPU:1, one launch (start us, length us, event | category | flops | bytes accessed | tf_op | source)
XLA Modules:
  0.0 46.5 jit_solution(13841902597900861871)
XLA Ops:
  0.7 44.5 %shard_map.55 = (bf16[16,256,256]{2,1,0:T(8,128)(2,1)S(1)}, bf16[13,256,256]{2,1,0:T(8,128)(2,1)S(1)}, bf16[3072,256]{1,0:T(8,128)(2,1)S(1)}, bf16[256,256]{1,0:...) custom-call(s32[1]{0:T(128)S(6)} %copy.6.counts_ref, s32[12]{0:T(128)} %deltas_ref.1, ...), custom_call_target="tpu_custom_call" | custom-call | flops 12884901888 | bytes 7340032 | tf_op jit(solution)/shard_map/pallas_call | solution.py:296
  45.2 1.3 %shard_map.56 = bf16[16,256,256]{2,1,0:T(8,128)(2,1)} custom-call(s32[12]{0:T(128)S(4)} %get-tuple-element.11.reads, bf16[256,256]{1,0:T(8,128)(2,1)S(1)} %get-tuple-element.12.late, bf16[13,256,256]{2,1,0:T(8,128)(2,1)S(1)} %get-tuple-element.13.left, bf16[3072,256]{1,0:T(8,128)(2,1)S(1)} %get-tuple-element.14.right_t, ...), custom_call_target="tpu_custom_call" | custom-call | flops 805306368 | bytes 2097152 | tf_op jit(solution)/shard_map/pallas_call | solution.py:330

commit v9 on v8

--- a/solution.py
+++ b/solution.py
@@ -28,10 +28,17 @@
     last = out_ref.shape[0] - 1
     width = left.shape[1]
     slots = left.shape[0] - 1
-    done_copy = pltpu.make_async_copy(
-        done_ref.at[pl.ds(0, last)], out_ref.at[pl.ds(0, last)], done_sem
-    )
-    done_copy.start()
+    pieces = done_sem.shape[0]
+    edges = [last * piece // pieces for piece in range(pieces + 1)]
+    done_copies = [
+        pltpu.make_async_copy(
+            done_ref.at[pl.ds(start, stop - start)], out_ref.at[pl.ds(start, stop - start)],
+            done_sem.at[piece],
+        )
+        for piece, (start, stop) in enumerate(zip(edges, edges[1:]))
+    ]
+    for copy in done_copies:
+        copy.start()
 
     for place in range(slots):
         order[place] = slots
@@ -63,7 +70,8 @@
 
     last_copy = pltpu.make_async_copy(result, out_ref.at[last], last_sem)
     last_copy.start()
-    done_copy.wait()
+    for copy in done_copies:
+        copy.wait()
     last_copy.wait()
 
 
@@ -337,7 +345,7 @@
             pltpu.VMEM((width, slots * width), bf16),
             pltpu.VMEM((slots * width, width), bf16),
             pltpu.VMEM((width, width), bf16),
-            pltpu.SemaphoreType.DMA,
+            pltpu.SemaphoreType.DMA((5,)),
             pltpu.SemaphoreType.DMA,
         ],
         compiler_params=pltpu.CompilerParams(vmem_limit_bytes=48 * 2**20),

time: 46.6 us -> 46.7 us (level)
  no operation moved by 1% of the time
where the time goes in v9:
time: 46.7 us; the launch traced here: 46.5 us
  Pallas kernels  45.9 us (98%)
  between operations  0.66 us (1%)
    pallas_call x1, Pallas kernels, on_device(): pl.pallas_call(functools.partial(kernel, sectors), out_shape=(pltpu.VMEM(...  44.5 us
    pallas_call x1, Pallas kernels, on_device(): pl.pallas_call(finish, out_shape=jax.ShapeDtypeStruct(block, bf16), in_sp...  1.36 us

profile of v9, /device:TPU:1, one launch (start us, length us, event | category | flops | bytes accessed | tf_op | source)
XLA Modules:
  0.0 46.5 jit_solution(2419679607999020588)
XLA Ops:
  0.7 44.5 %shard_map.55 = (bf16[16,256,256]{2,1,0:T(8,128)(2,1)S(1)}, bf16[13,256,256]{2,1,0:T(8,128)(2,1)S(1)}, bf16[3072,256]{1,0:T(8,128)(2,1)S(1)}, bf16[256,256]{1,0:...) custom-call(s32[1]{0:T(128)S(6)} %copy.6.counts_ref, s32[12]{0:T(128)} %deltas_ref.1, ...), custom_call_target="tpu_custom_call" | custom-call | flops 12884901888 | bytes 7340032 | tf_op jit(solution)/shard_map/pallas_call | solution.py:304
  45.2 1.4 %shard_map.56 = bf16[16,256,256]{2,1,0:T(8,128)(2,1)} custom-call(s32[12]{0:T(128)S(4)} %get-tuple-element.11.reads, bf16[256,256]{1,0:T(8,128)(2,1)S(1)} %get-tuple-element.12.late, bf16[13,256,256]{2,1,0:T(8,128)(2,1)S(1)} %get-tuple-element.13.left, bf16[3072,256]{1,0:T(8,128)(2,1)S(1)} %get-tuple-element.14.right_t, ...), custom_call_target="tpu_custom_call" | custom-call | flops 805306368 | bytes 2097152 | tf_op jit(solution)/shard_map/pallas_call | solution.py:338

commit v10 on v9

--- a/solution.py
+++ b/solution.py
@@ -92,23 +92,23 @@
     row, place = lax.div(me, 4), lax.rem(me, 4)
     above, below = row < rows - 1, jnp.logical_and(row > 0, row < rows)
     up_source = jnp.logical_and(place == 3, above)
-    up_relay = jnp.logical_and(place == 1, above)
+    up_relay = jnp.logical_and(place == 0, above)
     down_source = jnp.logical_and(place == 0, below)
-    down_relay = jnp.logical_and(place == 2, below)
+    down_relay = jnp.logical_and(place == 3, below)
     up_share = lax.div(roots * (rows - 1 - row), max(rows, 1))
     down_share = lax.div(roots * row, max(rows, 1))
     up_detour = jnp.where(up_source, up_share, 0)
     down_detour = jnp.where(down_source, down_share, 0)
     forwards = jnp.where(up_relay, up_share, jnp.where(down_relay, down_share, 0))
-    ahead = jnp.where(up_relay, me + 3, jnp.where(down_relay, me - 3, me))
+    ahead = jnp.where(up_relay, me + 4, jnp.where(down_relay, me - 4, me))
 
     partners = [(has_low, me - 1), (has_high, me + 1)]
     if rows:
         partners += [
-            (up_source, me - 2), (up_source, me + 3),
-            (down_source, me + 2), (down_source, me - 3),
-            (up_relay, me + 2), (up_relay, me + 3),
-            (down_relay, me - 2), (down_relay, me - 3),
+            (up_source, me - 3), (up_source, me + 4),
+            (down_source, me + 3), (down_source, me - 4),
+            (up_relay, me + 3), (up_relay, me + 4),
+            (down_relay, me - 3), (down_relay, me - 4),
         ]
     barrier = pltpu.get_barrier_semaphore()
     for present, partner in partners:
@@ -168,11 +168,11 @@
         if rows:
             @pl.when(step < up_detour)
             def _():
-                aside(roots - up_detour + step, step, 0, me - 2).start()
+                aside(roots - up_detour + step, step, 0, me - 3).start()
 
             @pl.when(step < down_detour)
             def _():
-                aside(roots - down_detour + step, step, 1, me + 2).start()
+                aside(roots - down_detour + step, step, 1, me + 3).start()
 
     @pl.when(jnp.logical_not(has_low))
     def _():

time: 46.7 us -> 46.7 us (level)
  no operation moved by 1% of the time
where the time goes in v10:
time: 46.7 us; the launch traced here: 46.5 us
  Pallas kernels  45.9 us (98%)
  between operations  0.66 us (1%)
    pallas_call x1, Pallas kernels, on_device(): pl.pallas_call(functools.partial(kernel, sectors), out_shape=(pltpu.VMEM(...  44.5 us
    pallas_call x1, Pallas kernels, on_device(): pl.pallas_call(finish, out_shape=jax.ShapeDtypeStruct(block, bf16), in_sp...  1.36 us

profile of v10, /device:TPU:1, one launch (start us, length us, event | category | flops | bytes accessed | tf_op | source)
XLA Modules:
  0.0 46.5 jit_solution(11834219865548844042)
XLA Ops:
  0.7 44.5 %shard_map.55 = (bf16[16,256,256]{2,1,0:T(8,128)(2,1)S(1)}, bf16[13,256,256]{2,1,0:T(8,128)(2,1)S(1)}, bf16[3072,256]{1,0:T(8,128)(2,1)S(1)}, bf16[256,256]{1,0:...) custom-call(s32[1]{0:T(128)S(6)} %copy.6.counts_ref, s32[12]{0:T(128)} %deltas_ref.1, ...), custom_call_target="tpu_custom_call" | custom-call | flops 12884901888 | bytes 7340032 | tf_op jit(solution)/shard_map/pallas_call | solution.py:304
  45.2 1.4 %shard_map.56 = bf16[16,256,256]{2,1,0:T(8,128)(2,1)} custom-call(s32[12]{0:T(128)S(4)} %get-tuple-element.11.reads, bf16[256,256]{1,0:T(8,128)(2,1)S(1)} %get-tuple-element.12.late, bf16[13,256,256]{2,1,0:T(8,128)(2,1)S(1)} %get-tuple-element.13.left, bf16[3072,256]{1,0:T(8,128)(2,1)S(1)} %get-tuple-element.14.right_t, ...), custom_call_target="tpu_custom_call" | custom-call | flops 805306368 | bytes 2097152 | tf_op jit(solution)/shard_map/pallas_call | solution.py:338
